TPU v7x, 32 devices: a whole 2x2x4 slice. The times are simulated.
32 devices in a mesh: groups: 2 (over y), fluid: 4 (over z), metal: 2 (over x), span: 2 (over core).
Axes of the slice: x: 2, y: 2, z: 4, core: 2. Of those that a mesh axis runs over, the one named last changes fastest.
Arguments:
- fluid_temp: bfloat16 [64, 8, 128, 512], P(('groups', 'fluid', 'metal'), None, None, 'span'), parts along dimension 0, may hold values from -6 to 6
- wall_old: float32 [64, 128, 512], P(('groups', 'fluid', 'metal'), None, 'span'), parts along dimension 0, may hold values from -6 to 6
- conductance: float32 [64, 128], P(('groups', 'fluid', 'metal')), parts along dimension 0, may hold values from 0.5 to 4
- valid_rows: int32 [64], P(('groups', 'fluid', 'metal')), parts along dimension 0, may hold values from 64 to 128
- face_owner: int32 [64, 128, 1], P(('groups', 'fluid', 'metal')), parts along dimension 0, may hold values from 0 to 3; in each aligned block of 512 rows (0 to 511, 512 to 1023, ..., all dimensions but the last counted through in order) at most 192 rows name the same one
- face_slot: int32 [64, 128], P(('groups', 'fluid', 'metal')), parts along dimension 0, may hold values from 0 to 511
- response: bfloat16 [4, 1024, 1024], P('fluid', 'metal'), as said below
- coolant: float32 [4, 1024], P('fluid', 'metal'), may hold values from 0.5 to 1.5
- flux_old: float32 [8, 1024, 512], P(('groups', 'fluid'), 'metal', 'span'), parts along dimension 0, may hold values from -6 to 6
Outputs:
- flux_avg: float32 [8, 1024, 512], P(('groups', 'fluid'), 'metal', 'span'), parts along dimension 0
- metal_wall: float32 [8, 1024, 512], P(('groups', 'fluid'), 'metal', 'span'), parts along dimension 0
- wall_new: float32 [64, 128, 512], P(('groups', 'fluid', 'metal'), None, 'span'), parts along dimension 0
There are 2 independent parts, one for each index of `groups`. A program takes and returns all parts, laid end to end along the dimension named above; an argument that names none is the same for every part. Nothing has to cross between parts.
Inputs may be any that keep to these rules, and one draw needn't show every extreme that they name: `face_owner`: among the 512 cells of one device's blocks (padded ones included) at most 192 name one owner, and in some device's cells some owner is named exactly 192 times. response[o] is symmetric: response[o, i, j] = response[o, j, i].
All inputs are finite; a program needn't handle non-finite values.
Results may differ from a plain program's by a relative error of at most 0.0017.
Values may be sent and summed in bfloat16 or wider, within the bound.
A program may use at most 64 MiB of HBM per device.

v0:
```python
import jax
import jax.numpy as jnp
from jax import lax
from jax.sharding import PartitionSpec as P

average_weight = 0.3
span_mix = 0.25
relaxation = 0.5


def with_halo(block, sides, width):
    for axis, dim in sides:
        count = lax.axis_size(axis)
        forward = [(i, i + 1) for i in range(count - 1)]
        forward.append((count - 1, 0))
        backward = [(target, source) for source, target in forward]
        low = lax.ppermute(
            lax.slice_in_dim(block, block.shape[dim] - width, None, axis=dim), axis, forward
        )
        high = lax.ppermute(lax.slice_in_dim(block, 0, width, axis=dim), axis, backward)
        block = jnp.concatenate([low, block, high], axis=dim)
    return block


def body(
    fluid_temp,
    wall_old,
    conductance,
    valid_rows,
    face_owner,
    face_slot,
    response,
    coolant,
    flux_old,
):
    blocks, layers, cells, span_dev = fluid_temp.shape
    row_count = blocks * cells
    fluid_count = lax.axis_size("fluid")
    capacity = 3 * row_count // (2 * fluid_count)
    slots_dev = response.shape[1]
    level = jnp.arange(layers, dtype=jnp.float32)
    weights = 2.0 * (layers - level) / (layers * (layers + 1.0))
    near_wall = jnp.sum(fluid_temp.astype(jnp.float32) * weights[None, :, None, None], axis=1)
    active = jnp.arange(cells, dtype=jnp.int32)[None, :] < valid_rows[:, None]
    heat_flux = jnp.where(active[:, :, None], conductance[:, :, None] * (near_wall - wall_old), 0.0)
    flat_flux = heat_flux.reshape(row_count, span_dev)
    active_rows = active.reshape(row_count)
    destination = face_owner.reshape(row_count)
    chosen = (
        destination[:, None] == jnp.arange(fluid_count, dtype=jnp.int32)[None, :]
    ) & active_rows[:, None]
    ordinal = jnp.sum(
        jnp.where(chosen, jnp.cumsum(chosen.astype(jnp.int32), axis=0) - 1, 0), axis=1
    )
    position = jnp.where(active_rows, destination * capacity + ordinal, fluid_count * capacity)
    outgoing = (
        jnp.zeros((fluid_count * capacity, span_dev), jnp.float32)
        .at[position]
        .set(flat_flux, mode="drop")
    )
    slot_values = (
        jnp.full((fluid_count * capacity,), -1.0, jnp.float32)
        .at[position]
        .set(face_slot.reshape(row_count).astype(jnp.float32), mode="drop")
    )
    incoming, arrived = (
        lax.all_to_all(
            outgoing.reshape(fluid_count, capacity, span_dev),
            "fluid",
            split_axis=0,
            concat_axis=0,
            tiled=True,
        ),
        lax.all_to_all(
            slot_values.reshape(fluid_count, capacity),
            "fluid",
            split_axis=0,
            concat_axis=0,
            tiled=True,
        ),
    )
    arrived_index = arrived.reshape(-1).astype(jnp.int32)
    slot_index = jnp.where(arrived_index >= 0, arrived_index, slots_dev)
    summed = (
        jnp.zeros((slots_dev + 1, span_dev), jnp.float32)
        .at[slot_index]
        .add(incoming.reshape(-1, span_dev))[:slots_dev]
    )
    flux_avg = (1.0 - average_weight) * flux_old[0] + average_weight * summed
    flux_low = flux_avg.astype(jnp.bfloat16)
    local_response = response[0]
    temp_rise = lax.psum_scatter(
        lax.dot_general(
            local_response, flux_low, (((0,), (0,)), ((), ())), preferred_element_type=jnp.float32
        ),
        "metal",
        scatter_dimension=0,
        tiled=True,
    )
    slot_temp = coolant[0][:, None] + temp_rise
    padded = with_halo(slot_temp, (("span", 1),), 1)
    metal_wall = slot_temp + span_mix * (padded[:, 2:] - 2.0 * slot_temp + padded[:, :-2])
    extended = jnp.concatenate([metal_wall, jnp.zeros((1, span_dev), jnp.float32)], axis=0)
    lookup = extended[slot_index].reshape(fluid_count, capacity, span_dev)
    returned = lax.all_to_all(lookup, "fluid", split_axis=0, concat_axis=0, tiled=True)
    back_rows = jnp.concatenate(
        [returned.reshape(fluid_count * capacity, span_dev), jnp.zeros((1, span_dev), jnp.float32)],
        axis=0,
    )
    face_temp = back_rows[position].reshape(blocks, cells, span_dev)
    wall_new = jnp.where(
        active[:, :, None], (1.0 - relaxation) * wall_old + relaxation * face_temp, 0.0
    )
    return (flux_avg[None], metal_wall[None], wall_new)


def solution(mesh):
    in_specs = (
        P(("groups", "fluid", "metal"), None, None, "span"),
        P(("groups", "fluid", "metal"), None, "span"),
        P(("groups", "fluid", "metal"), None),
        P(("groups", "fluid", "metal")),
        P(("groups", "fluid", "metal"), None, None),
        P(("groups", "fluid", "metal"), None),
        P("fluid", "metal", None),
        P("fluid", "metal"),
        P(("groups", "fluid"), "metal", "span"),
    )
    out_specs = (
        P(("groups", "fluid"), "metal", "span"),
        P(("groups", "fluid"), "metal", "span"),
        P(("groups", "fluid", "metal"), None, "span"),
    )
    return jax.shard_map(body, mesh=mesh, in_specs=in_specs, out_specs=out_specs, check_vma=False)
```

profile of v0, /device:TPU:0, one launch (start us, length us, event | category | flops | bytes accessed | tf_op | source)
XLA Modules:
  0.0 119.7 jit_solution(16695485057002584425)
XLA Ops:
  7.2 0.8 fusion.24
  8.0 0.7 fusion.17
  8.7 1.2 %reduce-window.6 = s32[4,4,128]{2,1,0:T(4,128)S(1)} reduce-window(s32[4,4,128]{2,1,0:T(4,128)S(1)} %fusion.17, s32[]{:T(128)} %constant.20.clone.1), window={size=1x1x128 pad=0_0x0_0x127_0}, to_apply=%region_0.0 | reduce-window | flops 260096 | bytes 16388 | tf_op jit(solution)/shard_map/reduce-window
  10.4 0.7 fusion.14
  11.1 0.7 compare_select_fusion.2
  11.8 0.7 convert_bitcast_fusion
  12.5 2.4 %scatter_custom_fusion = f32[768]{0:T(1024)S(1)} fusion(s32[512]{0:T(512)S(1)} %bitcast.69, f32[512]{0:T(512)S(1)} %convert_bitcast_fusion, f32[]{:T(128)} %constant.18.clone.1), kind=kCustom, calls=%fused_computation.47 | custom fusion | bytes 3076 | tf_op jit(solution)/shard_map/scatter | solution.py:64
  15.0 0.7 all_to_all.12
  15.6 6.3 %all-to-all-start = ((f32[4,1,192]{2,1,0:T(1,128)}), f32[4,1,192]{2,1,0:T(1,128)S(1)}, u32[]{:S(2)}, u32[]{:S(2)}) async-start(f32[4,1,192]{2,1,0:T(1,128)} %all_to_all.12), calls=%async_computation | async-start | bytes 8192 | tf_op jit(solution)/shard_map/all_to_all | solution.py:74
  22.0 2.1 %multiply_reduce_fusion = f32[4,128,256]{2,1,0:T(8,128)S(1)} fusion(bf16[4,8,128,256]{3,2,1,0:T(8,128)(2,1)} %param.9, f32[8]{0:T(128)S(1)} %subtract_multiply_fusion), kind=kLoop, calls=%fused_computation.5 | loop fusion | flops 3014656 | bytes 2621472 | tf_op jit(solution)/shard_map/reduce_sum | solution.py:43
  24.4 3.1 %scatter_custom_fusion.1 = f32[768,256]{1,0:T(8,128)} fusion(s32[512]{0:T(512)S(1)} %bitcast.70, f32[512,256]{1,0:T(8,128)S(1)} %bitcast.62, f32[]{:T(128)} %constant.17.clone.1), kind=kCustom, calls=%fused_computation.18 | custom fusion | bytes 786436 | tf_op jit(solution)/shard_map/scatter | solution.py:59
  27.5 5.1 %all-to-all-start.1 = ((f32[4,192,256]{2,1,0:T(8,128)}), f32[4,192,256]{2,1,0:T(8,128)S(1)}, u32[]{:S(2)}, u32[]{:S(2)}) async-start(f32[4,192,256]{2,1,0:T(8,128)} %bitcast.10), calls=%async_computation.1 | async-start | bytes 1572864 | tf_op jit(solution)/shard_map/all_to_all | solution.py:67
  32.7 19.4 %all-to-all-done.1 = f32[4,192,256]{2,1,0:T(8,128)S(1)} async-done(((f32[4,192,256]{2,1,0:T(8,128)}), f32[4,192,256]{2,1,0:T(8,128)S(1)}, u32[]{:S(2)}, u32[]{:S(2)}) %all-to-all-start.1) | async-done | bytes 786464 | tf_op jit(solution)/shard_map/all_to_all | solution.py:67
  52.1 6.3 %scatter_custom_fusion.2 = f32[513,256]{1,0:T(8,128)S(1)} fusion(s32[768]{0:T(1024)S(1)} %fusion.18, f32[768,256]{1,0:T(8,128)S(1)} %bitcast.61, f32[]{:T(128)} %constant.17.clone.1), kind=kCustom, calls=%fused_computation.20 | custom fusion | flops 196608 | bytes 525316 | tf_op jit(solution)/shard_map/scatter-add | solution.py:87
  58.5 1.5 %convolution_bitcast_fusion = f32[1024,256]{0,1:T(8,128)} fusion(bf16[1,512,1024]{2,1,0:T(8,128)(2,1)S(1)} %copy-done, f32[513,256]{1,0:T(8,128)S(1)} %scatter_custom_fusion.2, f32[1,512,256]{2,1,0:T(8,128)S(1)} %copy-done.3), kind=kOutput, calls=%fused_computation.6 | convolution fusion | flops 268959744 | bytes 3145728 | tf_op jit(solution)/shard_map/dot_general | solution.py:93
  60.0 19.2 %reduce-scatter.2.cloned.1.call-done = f32[512,256]{0,1:T(8,128)} async-done(((f32[1024,256]{0,1:T(8,128)}), f32[512,256]{0,1:T(8,128)}) %reduce-scatter.2.cloned.1.call-update) | async-done | bytes 524304 | tf_op jit(solution)/shard_map/reduce_scatter | solution.py:92
  79.2 1.1 broadcast_add_fusion
  82.1 2.9 %gather_fusion = f32[768,256]{1,0:T(8,128)} fusion(f32[513,256]{1,0:T(8,128)S(1)} %concatenate.15.clone, s32[1024]{0:T(1024)S(1)} %pad_clamp_fusion.1), kind=kCustom, calls=%fused_computation | custom fusion | bytes 1575936 | tf_op jit(solution)/shard_map/gather | solution.py:104
  85.0 4.6 %all-to-all-start.2 = ((f32[4,192,256]{2,1,0:T(8,128)}), f32[4,192,256]{2,1,0:T(8,128)S(1)}, u32[]{:S(2)}, u32[]{:S(2)}) async-start(f32[4,192,256]{2,1,0:T(8,128)} %bitcast.17), calls=%async_computation.3 | async-start | bytes 1572864 | tf_op jit(solution)/shard_map/all_to_all | solution.py:105
  89.6 2.0 %fusion.12 = f32[1,512,256]{2,1,0:T(8,128)} fusion(f32[513,256]{1,0:T(8,128)S(1)} %scatter_custom_fusion.2, f32[1,512,256]{2,1,0:T(8,128)} %param.17), kind=kLoop, calls=%fused_computation.24 | loop fusion | flops 393216 | bytes 1572864 | tf_op jit(solution)/shard_map/broadcast_in_dim | solution.py:114
  91.8 1.0 copy.15
  92.8 17.5 %all-to-all-done.2 = f32[4,192,256]{2,1,0:T(8,128)S(1)} async-done(((f32[4,192,256]{2,1,0:T(8,128)}), f32[4,192,256]{2,1,0:T(8,128)S(1)}, u32[]{:S(2)}, u32[]{:S(2)}) %all-to-all-start.2) | async-done | bytes 786464 | tf_op jit(solution)/shard_map/all_to_all | solution.py:105
  110.3 1.6 %gather_fusion.1 = f32[512,256]{1,0:T(8,128)S(1)} fusion(f32[769,256]{1,0:T(8,128)S(1)} %concatenate.16, s32[1024]{0:T(1024)S(1)} %pad_clamp_fusion), kind=kCustom, calls=%fused_computation.1 | custom fusion | bytes 1050624 | tf_op jit(solution)/shard_map/gather | solution.py:110
  111.9 0.9 multiply_select_fusion
  (36 shorter events, 2.9 us)
Async XLA Ops:
  7.2 51.3 %copy-start = (bf16[1,512,1024]{2,1,0:T(8,128)(2,1)S(1)}, bf16[1,512,1024]{2,1,0:T(8,128)(2,1)}, u32[]{:S(2)}) copy-start(bf16[1,512,1024]{2,1,0:T(8,128)(2,1)} %param.15) | copy-start | bytes 3145732
  7.2 16.9 %copy-start.1 = (f32[4,128,256]{2,1,0:T(8,128)S(1)}, f32[4,128,256]{2,1,0:T(8,128)}, u32[]{:S(2)}) copy-start(f32[4,128,256]{2,1,0:T(8,128)} %param.10) | copy-start | bytes 1572868
  7.2 16.9 %copy-start.4 = (f32[4,128]{1,0:T(4,128)S(1)}, f32[4,128]{1,0:T(4,128)}, u32[]{:S(2)}) copy-start(f32[4,128]{1,0:T(4,128)} %param.11) | copy-start | bytes 6148
  15.6 11.9 %all-to-all-start = ((f32[4,1,192]{2,1,0:T(1,128)}), f32[4,1,192]{2,1,0:T(1,128)S(1)}, u32[]{:S(2)}, u32[]{:S(2)}) async-start(f32[4,1,192]{2,1,0:T(1,128)} %all_to_all.12), calls=%async_computation | async-start | bytes 8192 | tf_op jit(solution)/shard_map/all_to_all | solution.py:74
  24.1 34.3 %copy-start.3 = (f32[1,512,256]{2,1,0:T(8,128)S(1)}, f32[1,512,256]{2,1,0:T(8,128)}, u32[]{:S(2)}) copy-start(f32[1,512,256]{2,1,0:T(8,128)} %param.17) | copy-start | bytes 1572868
  27.5 24.6 %all-to-all-start.1 = ((f32[4,192,256]{2,1,0:T(8,128)}), f32[4,192,256]{2,1,0:T(8,128)S(1)}, u32[]{:S(2)}, u32[]{:S(2)}) async-start(f32[4,192,256]{2,1,0:T(8,128)} %bitcast.10), calls=%async_computation.1 | async-start | bytes 1572864 | tf_op jit(solution)/shard_map/all_to_all | solution.py:67
  32.6 46.6 %reduce-scatter.2.cloned.1.call-start = ((), (), s32[]{:S(2)}) async-start(), calls=%async_computation.4 | async-start | bytes 1572864 | tf_op jit(solution)/shard_map/reduce_scatter | solution.py:92
  58.5 20.7 %copy-start.5 = (f32[1,512]{1,0:T(1,128)S(1)}, f32[1,512]{1,0:T(1,128)}, u32[]{:S(2)}) copy-start(f32[1,512]{1,0:T(1,128)} %param.16) | copy-start | bytes 6148
  80.3 1.2 %collective-permute-start.1 = (f32[512,1]{0,1:T(1,128)S(1)}, f32[512,1]{0,1:T(1,128)S(1)}, u32[]{:S(2)}, u32[]{:S(2)}) collective-permute-start(f32[512,1]{0,1:T(1,128)S(1)} %get-tuple-element.12), channel_id=1, source_target_pairs={{0,1},{1,0},{2,3},{3,2},{4,5},{5,4},{6,7},{7,6},{8,9},{9,8},{10,11... | collective-permute-start | bytes 6152 | tf_op jit(solution)/shard_map/ppermute | solution.py:17
  80.4 1.3 %collective-permute-start = (f32[512,1]{0,1:T(1,128)S(1)}, f32[512,1]{0,1:T(1,128)S(1)}, u32[]{:S(2)}, u32[]{:S(2)}) collective-permute-start(f32[512,1]{0,1:T(1,128)S(1)} %get-tuple-element.11), channel_id=1, source_target_pairs={{1,0},{0,1},{3,2},{2,3},{5,4},{4,5},{7,6},{6,7},{9,8},{8,9},{11,10... | collective-permute-start | bytes 6152 | tf_op jit(solution)/shard_map/ppermute | solution.py:20
  85.0 25.2 %all-to-all-start.2 = ((f32[4,192,256]{2,1,0:T(8,128)}), f32[4,192,256]{2,1,0:T(8,128)S(1)}, u32[]{:S(2)}, u32[]{:S(2)}) async-start(f32[4,192,256]{2,1,0:T(8,128)} %bitcast.17), calls=%async_computation.3 | async-start | bytes 1572864 | tf_op jit(solution)/shard_map/all_to_all | solution.py:105
  110.3 1.6 %copy-start.2 = (f32[4,128,256]{2,1,0:T(8,128)S(1)}, f32[4,128,256]{2,1,0:T(8,128)}, u32[]{:S(2)}) copy-start(f32[4,128,256]{2,1,0:T(8,128)} %param.10) | copy-start | bytes 1572868
Sparse Core Ops, SparseCore 0:
  60.1 19.0 reduce-scatter.1
where the time goes:
time: 120 us
  waiting for transfers between devices  56.9 us (47%)
  other arithmetic  18.1 us (15%)
  starting transfers between devices  16.6 us (14%)
  between operations  14.2 us (12%)
  local copies, waits for them, and re-layouts  12.3 us (10%)
  matrix products  1.51 us (1%)
    all_to_all x1, waiting for transfers between devices, body(): lax.all_to_all(outgoing.reshape(fluid_count, capacity, span_dev), 'fluid'...  19.4 us
    reduce_scatter x1, waiting for transfers between devices, body(): lax.psum_scatter(lax.dot_general(local_response, flux_low, (((0,), (0,)),...  19.2 us
    all_to_all x1, waiting for transfers between devices, body(): lax.all_to_all(lookup, 'fluid', split_axis=0, concat_axis=0, tiled=True)  17.5 us
    all_to_all x1, starting transfers between devices, body(): lax.all_to_all(slot_values.reshape(fluid_count, capacity), 'fluid', split...  6.32 us
    scatter-add x1, other arithmetic, body(): summed = jnp.zeros((slots_dev + 1, span_dev), jnp.float32).at[slot_index]...  6.27 us
    all_to_all x1, starting transfers between devices, body(): lax.all_to_all(outgoing.reshape(fluid_count, capacity, span_dev), 'fluid'...  5.08 us
    all_to_all x1, starting transfers between devices, body(): lax.all_to_all(lookup, 'fluid', split_axis=0, concat_axis=0, tiled=True)  4.6 us
    scatter x1, local copies, waits for them, and re-layouts, body(): outgoing = jnp.zeros((fluid_count * capacity, span_dev), jnp.float32).at[...  3.12 us
  transfers between devices with their start and end apart: 6, of which 5 were waited for; matrix products, arithmetic and copies ran while one was open for 7% of the time, Pallas kernels for 0%

commit v1 on v0

v1 whole, which is shorter than its diff:
```python
import functools

import jax
import jax.numpy as jnp
from jax import lax
from jax.experimental import pallas as pl
from jax.experimental.pallas import tpu as pltpu
from jax.sharding import PartitionSpec as P

average_weight = 0.3
span_mix = 0.25
relaxation = 0.5
code_limit = 32512.0
MESH = pl.DeviceIdType.MESH
f32, bf16, i32, i16 = jnp.float32, jnp.bfloat16, jnp.int32, jnp.int16


def mm(a, b):
    return jnp.dot(a, b, preferred_element_type=f32)


def to_column(row):
    eye = lax.broadcasted_iota(i32, (128, 128), 0) == lax.broadcasted_iota(i32, (128, 128), 1)
    return jnp.concatenate(
        [
            jnp.sum(jnp.where(eye, row[:, i : i + 128], 0.0), axis=1, keepdims=True)
            for i in range(0, row.shape[1], 128)
        ],
        axis=0,
    )


def encode(x):
    top = jnp.maximum(jnp.max(jnp.abs(x), keepdims=True), 1e-30)
    code = jnp.floor(x * (code_limit / top) + 0.5)
    return code, top * (1.0 / code_limit)


def code_parts(code):
    high = jnp.floor(code * (1.0 / 256.0) + 0.5)
    return jnp.concatenate([high, code - 256.0 * high], axis=1).astype(bf16)


def from_parts(both):
    half = both.shape[1] // 2
    return 256.0 * both[:, :half] + both[:, half:]


def value_parts(x):
    high = x.astype(bf16)
    return jnp.concatenate([high, (x - high.astype(f32)).astype(bf16)], axis=1)


def add_parts(both):
    half = both.shape[1] // 2
    return both[:, :half] + both[:, half:]


def pick(x, chunk):
    n = x.shape[1]
    if chunk == 0:
        return jnp.concatenate([x[:, 3 * n // 4 :], x[:, : n // 4]], axis=1)
    return x[:, n // 4 : 3 * n // 4]


def unpick(edge, middle):
    half = edge.shape[1] // 2
    return jnp.concatenate([edge[:, half:], middle, edge[:, :half]], axis=1)


def smooth(edge, middle, other):
    width = edge.shape[1]
    x = jnp.concatenate([edge, middle], axis=1)
    low = pltpu.roll(x, 1, 1)
    high = pltpu.roll(x, 2 * width - 1, 1)
    lane = lax.broadcasted_iota(i32, edge.shape, 1)
    low_edge = jnp.where(lane == width // 2, pltpu.roll(other, 1, 1), low[:, :width])
    high_edge = jnp.where(lane == width // 2 - 1, pltpu.roll(other, width - 1, 1), high[:, :width])
    new_edge = edge + span_mix * (high_edge - 2.0 * edge + low_edge)
    new_middle = middle + span_mix * (high[:, width:] - 2.0 * middle + low[:, width:])
    return unpick(new_edge, new_middle)


def kernel(
    fluids, metals, cap,
    valid, fluid_in, wall_in, cond, owner, slot, resp_in, cool, old_in,
    favg_out, mwall_out, wnew_out,
    fluid_v, wall_v, resp_v, old_v,
    pack, unpack, spread, fetch,
    meta_s, meta_r, flux_s, flux_r, fstep_s, fstep_r,
    low_v, temp_v, halo_t, back_s, back_r, bstep_s, bstep_r, face_v, halo_f,
    favg_v, mwall_v, wnew_v,
    local_sem, meta_sem, flux_sem, fstep_sem, low_sem, halo_sem, back_sem, bstep_sem,
):
    blocks, layers, cells, span_dev = fluid_v.shape
    rows = blocks * cells
    slots = resp_v.shape[0]
    width = span_dev // 2
    me_f, me_m, me_s = lax.axis_index("fluid"), lax.axis_index("metal"), lax.axis_index("span")
    up = [None] + [lax.rem(me_f + r, fluids) for r in range(1, fluids)]
    down = [None] + [lax.rem(me_f + fluids - r, fluids) for r in range(1, fluids)]
    across = [None] + [lax.rem(me_m + r, metals) for r in range(1, metals)]
    mate = 1 - me_s

    loads = [
        pltpu.make_async_copy(src, dst, local_sem.at[i])
        for i, (src, dst) in enumerate(
            ((fluid_in, fluid_v), (wall_in, wall_v), (old_in, old_v), (resp_in, resp_v))
        )
    ]
    for load in loads:
        load.start()

    barrier = pltpu.get_barrier_semaphore()
    for r in range(1, fluids):
        pl.semaphore_signal(barrier, inc=1, device_id={"fluid": up[r]}, device_id_type=MESH)
    for r in range(1, metals):
        pl.semaphore_signal(barrier, inc=1, device_id={"metal": across[r]}, device_id_type=MESH)
    pl.semaphore_signal(barrier, inc=1, device_id={"span": mate}, device_id_type=MESH)

    def remote(src, dst, sems, place, where):
        return pltpu.make_async_remote_copy(
            src_ref=src, dst_ref=dst, send_sem=sems.at[(0, *place)], recv_sem=sems.at[(1, *place)],
            device_id=where, device_id_type=MESH,
        )

    away = jnp.concatenate([owner[b : b + 1, :] for b in range(blocks)], axis=1) - me_f
    away = jnp.where(away < 0, away + fluids, away)
    cell = lax.broadcasted_iota(i32, (1, cells), 1)
    live = jnp.concatenate([(cell < valid[b]).astype(i32) for b in range(blocks)], axis=1)
    away = jnp.where(live > 0, away, -1)
    lines = -(-fluids // 16) * 16
    chosen = lax.broadcasted_iota(i32, (lines, rows), 0) == away
    before = lax.broadcasted_iota(i32, (rows, rows), 0) < lax.broadcasted_iota(i32, (rows, rows), 1)
    earlier = mm(chosen.astype(f32).astype(bf16), before.astype(f32).astype(bf16))
    ordinal = jnp.sum(jnp.where(chosen, earlier, 0.0), axis=0, keepdims=True)
    place = jnp.where(away >= 0, away.astype(f32) * cap + ordinal, -1.0)
    total = fluids * cap
    pack[...] = (
        lax.broadcasted_iota(i32, (total, rows), 0).astype(f32) == place
    ).astype(f32).astype(bf16)
    place_col = to_column(place)
    unpack[...] = (
        lax.broadcasted_iota(i32, (rows, total), 1).astype(f32) == place_col
    ).astype(f32).astype(bf16)
    slot_row = jnp.concatenate([slot[b : b + 1, :] for b in range(blocks)], axis=1)
    line = lax.broadcasted_iota(i32, (16, rows), 0)
    halves = jnp.where(line == 0, slot_row // 256, jnp.where(line == 1, slot_row % 256, 0))
    packed_slots = mm(halves.astype(f32).astype(bf16), unpack[...])
    packed_slots = 256.0 * packed_slots[0:1] + packed_slots[1:2]
    for r in range(fluids):
        meta_s[r, :, 0:cap] = jnp.broadcast_to(packed_slots[:, r * cap : (r + 1) * cap], (8, cap))

    pl.semaphore_wait(barrier, fluids + metals - 1)
    sends = []

    def send(copy):
        copy.start()
        sends.append(copy)
        return copy

    metas = [
        send(remote(meta_s.at[r], meta_r.at[r], meta_sem, (r,), {"fluid": up[r]}))
        for r in range(1, fluids)
    ]

    loads[0].wait()
    loads[1].wait()
    weights = [2.0 * (layers - l) / (layers * (layers + 1.0)) for l in range(layers)]
    flux = []
    for b in range(blocks):
        near = weights[0] * fluid_v[b, 0].astype(f32)
        for l in range(1, layers):
            near = near + weights[l] * fluid_v[b, l].astype(f32)
        gain = to_column(cond[b : b + 1, :])
        lives = lax.broadcasted_iota(i32, (cells, 1), 0) < valid[b]
        flux.append(
            jnp.where(lives, gain * (near - wall_v[b * cells : (b + 1) * cells, :]), 0.0)
        )
    flux = jnp.concatenate(flux, axis=0)

    fluxes, fsteps = [], []
    for c in range(2):
        code, step = encode(pick(flux, c))
        fstep_s[c] = jnp.broadcast_to(step, (8, 128))
        packed = from_parts(mm(pack[...], code_parts(code))).astype(i32).astype(i16)
        for r in range(fluids):
            dst = flux_r if r == 0 else flux_s
            dst[c, r] = packed[r * cap : (r + 1) * cap]
        fsteps.append(
            [
                send(remote(fstep_s.at[c], fstep_r.at[c, r], fstep_sem, (c, r), {"fluid": up[r]}))
                for r in range(1, fluids)
            ]
        )
        fluxes.append(
            [
                send(remote(flux_s.at[c, r], flux_r.at[c, r], flux_sem, (c, r), {"fluid": up[r]}))
                for r in range(1, fluids)
            ]
        )

    for copy in metas:
        copy.wait_recv()
    arrived = jnp.concatenate(
        [packed_slots[:, 0:cap]] + [meta_r[r, 0:1, 0:cap] for r in range(1, fluids)], axis=1
    )
    spread[...] = (
        lax.broadcasted_iota(i32, (slots, total), 0).astype(f32) == arrived
    ).astype(f32).astype(bf16)
    fetch[...] = (
        lax.broadcasted_iota(i32, (total, slots), 1).astype(f32) == to_column(arrived)
    ).astype(f32).astype(bf16)
    cool_col = to_column(cool[...])
    loads[2].wait()
    loads[3].wait()

    averages, backs, bsteps = [], [], []
    for c in range(2):
        for copy in fsteps[c] + fluxes[c]:
            copy.wait_recv()
        incoming = jnp.concatenate(
            [
                flux_r[c, r].astype(i32).astype(f32)
                * (fstep_s[c, 0:1, :] if r == 0 else fstep_r[c, r, 0:1, :])
                for r in range(fluids)
            ],
            axis=0,
        )
        summed = add_parts(mm(spread[...], value_parts(incoming)))
        average = (1.0 - average_weight) * pick(old_v[...], c) + average_weight * summed
        averages.append(average)
        low_v[c, 0] = average.astype(bf16)
        lows = [
            send(remote(low_v.at[c, 0], low_v.at[c, r], low_sem, (c, r), {"metal": across[r]}))
            for r in range(1, metals)
        ]
        if c == 1:
            favg_v[...] = unpick(*averages)
            store_favg = pltpu.make_async_copy(favg_v, favg_out, local_sem.at[4])
            store_favg.start()
        temp = cool_col
        for r in range(metals):
            if r:
                lows[r - 1].wait_recv()
            stripe = lax.rem(me_m + metals - r, metals)
            columns = pl.ds(pl.multiple_of(stripe * slots, slots), slots)
            temp = temp + mm(resp_v[:, columns], low_v[c, r])
        temp_v[c] = temp
        if c == 0:
            edge_t = send(remote(temp_v.at[0], halo_t, halo_sem, (0,), {"span": mate}))
        code, step = encode(temp)
        bstep_s[c] = jnp.broadcast_to(step, (8, 128))
        found = from_parts(mm(fetch[...], code_parts(code))).astype(i32).astype(i16)
        for r in range(fluids):
            dst = back_r if r == 0 else back_s
            dst[c, r] = found[r * cap : (r + 1) * cap]
        bsteps.append(
            [
                send(remote(bstep_s.at[c], bstep_r.at[c, r], bstep_sem, (c, r), {"fluid": down[r]}))
                for r in range(1, fluids)
            ]
        )
        backs.append(
            [
                send(remote(back_s.at[c, r], back_r.at[c, r], back_sem, (c, r), {"fluid": down[r]}))
                for r in range(1, fluids)
            ]
        )

    edge_t.wait_recv()
    mwall_v[...] = smooth(temp_v[0], temp_v[1], halo_t[...])
    store_mwall = pltpu.make_async_copy(mwall_v, mwall_out, local_sem.at[5])
    store_mwall.start()

    for c in range(2):
        for copy in bsteps[c] + backs[c]:
            copy.wait_recv()
        returned = jnp.concatenate(
            [
                back_r[c, r].astype(i32).astype(f32)
                * (bstep_s[c, 0:1, :] if r == 0 else bstep_r[c, r, 0:1, :])
                for r in range(fluids)
            ],
            axis=0,
        )
        face_v[c] = add_parts(mm(unpack[...], value_parts(returned)))
        if c == 0:
            edge_f = send(remote(face_v.at[0], halo_f, halo_sem, (1,), {"span": mate}))
    edge_f.wait_recv()
    face = smooth(face_v[0], face_v[1], halo_f[...])
    for b in range(blocks):
        lives = lax.broadcasted_iota(i32, (cells, 1), 0) < valid[b]
        part = slice(b * cells, (b + 1) * cells)
        wnew_v[part, :] = jnp.where(
            lives, (1.0 - relaxation) * wall_v[part, :] + relaxation * face[part], 0.0
        )
    store_wnew = pltpu.make_async_copy(wnew_v, wnew_out, local_sem.at[6])
    store_wnew.start()
    for copy in sends:
        copy.wait_send()
    store_favg.wait()
    store_mwall.wait()
    store_wnew.wait()


def body(
    fluid_temp, wall_old, conductance, valid_rows, face_owner, face_slot, response, coolant, flux_old
):
    blocks, layers, cells, span_dev = fluid_temp.shape
    rows = blocks * cells
    fluids, metals = lax.axis_size("fluid"), lax.axis_size("metal")
    cap = -(-(3 * rows // (2 * fluids)) // 16) * 16
    lanes = -(-cap // 128) * 128
    slots = response.shape[1]
    width = span_dev // 2
    total = fluids * cap
    vmem = pl.BlockSpec(memory_space=pltpu.VMEM)
    smem = pl.BlockSpec(memory_space=pltpu.SMEM)
    anywhere = pl.BlockSpec(memory_space=pl.ANY)
    dma = pltpu.SemaphoreType.DMA
    out = pl.pallas_call(
        functools.partial(kernel, fluids, metals, cap),
        out_shape=[
            jax.ShapeDtypeStruct((slots, span_dev), f32),
            jax.ShapeDtypeStruct((slots, span_dev), f32),
            jax.ShapeDtypeStruct((rows, span_dev), f32),
        ],
        in_specs=[smem, anywhere, anywhere, vmem, vmem, vmem, anywhere, vmem, anywhere],
        out_specs=[anywhere] * 3,
        scratch_shapes=[
            pltpu.VMEM(fluid_temp.shape, bf16),
            pltpu.VMEM((rows, span_dev), f32),
            pltpu.VMEM(response.shape[1:], bf16),
            pltpu.VMEM((slots, span_dev), f32),
            pltpu.VMEM((total, rows), bf16),
            pltpu.VMEM((rows, total), bf16),
            pltpu.VMEM((slots, total), bf16),
            pltpu.VMEM((total, slots), bf16),
            pltpu.VMEM((fluids, 8, lanes), f32),
            pltpu.VMEM((fluids, 8, lanes), f32),
            pltpu.VMEM((2, fluids, cap, width), i16),
            pltpu.VMEM((2, fluids, cap, width), i16),
            pltpu.VMEM((2, 8, 128), f32),
            pltpu.VMEM((2, fluids, 8, 128), f32),
            pltpu.VMEM((2, metals, slots, width), bf16),
            pltpu.VMEM((2, slots, width), f32),
            pltpu.VMEM((slots, width), f32),
            pltpu.VMEM((2, fluids, cap, width), i16),
            pltpu.VMEM((2, fluids, cap, width), i16),
            pltpu.VMEM((2, 8, 128), f32),
            pltpu.VMEM((2, fluids, 8, 128), f32),
            pltpu.VMEM((2, rows, width), f32),
            pltpu.VMEM((rows, width), f32),
            pltpu.VMEM((slots, span_dev), f32),
            pltpu.VMEM((slots, span_dev), f32),
            pltpu.VMEM((rows, span_dev), f32),
            dma((7,)),
            dma((2, fluids)),
            dma((2, 2, fluids)),
            dma((2, 2, fluids)),
            dma((2, 2, metals)),
            dma((2, 2)),
            dma((2, 2, fluids)),
            dma((2, 2, fluids)),
        ],
        compiler_params=pltpu.CompilerParams(
            collective_id=0, has_side_effects=True, vmem_limit_bytes=48 * 1024 * 1024
        ),
    )(
        valid_rows,
        fluid_temp,
        wall_old.reshape(rows, span_dev),
        conductance,
        face_owner.reshape(blocks, cells),
        face_slot,
        response[0],
        coolant,
        flux_old[0],
    )
    return out[0][None], out[1][None], out[2].reshape(blocks, cells, span_dev)


def solution(mesh):
    in_specs = (
        P(("groups", "fluid", "metal"), None, None, "span"),
        P(("groups", "fluid", "metal"), None, "span"),
        P(("groups", "fluid", "metal"), None),
        P(("groups", "fluid", "metal")),
        P(("groups", "fluid", "metal"), None, None),
        P(("groups", "fluid", "metal"), None),
        P("fluid", "metal", None),
        P("fluid", "metal"),
        P(("groups", "fluid"), "metal", "span"),
    )
    out_specs = (
        P(("groups", "fluid"), "metal", "span"),
        P(("groups", "fluid"), "metal", "span"),
        P(("groups", "fluid", "metal"), None, "span"),
    )
    return jax.shard_map(body, mesh=mesh, in_specs=in_specs, out_specs=out_specs, check_vma=False)
```

time: 120 us -> 48.5 us (0.40)
  waiting for transfers between devices: 56.9 us -> 0 us
  Pallas kernels: 0 us -> 36.8 us
  other arithmetic: 18.1 us -> 0 us
  starting transfers between devices: 16.6 us -> 0 us
  between operations: 14.2 us -> 0.66 us
  local copies, waits for them, and re-layouts: 12.3 us -> 10.7 us
  matrix products: 1.51 us -> 0 us
    all_to_all x3 -> x0, waiting for transfers between devices: 36.9 us -> none  [the longest x1 19.4 us: body(): lax.all_to_all(outgoing.reshape(fluid_count, capacity, span_dev), 'fluid'...]
    pallas_call x0 -> x1, Pallas kernels: none -> 36.8 us  [body(): pl.pallas_call(functools.partial(kernel, fluids, metals, cap), out_shape=...]
    reduce_scatter x1 -> x0, waiting for transfers between devices: 19.2 us -> none  [body(): lax.psum_scatter(lax.dot_general(local_response, flux_low, (((0,), (0,)),...]
    all_to_all x3 -> x0, starting transfers between devices: 16 us -> none  [the longest x1 6.32 us: body(): lax.all_to_all(slot_values.reshape(fluid_count, capacity), 'fluid', split...]
    unnamed x14 -> x21, local copies, waits for them, and re-layouts: 1.23 us -> 10.7 us
    scatter-add x1 -> x0, other arithmetic: 6.27 us -> none  [body(): summed = jnp.zeros((slots_dev + 1, span_dev), jnp.float32).at[slot_index]...]
    scatter x2 -> x0, local copies, waits for them, and re-layouts: 5.56 us -> none  [the longest x1 3.12 us: body(): outgoing = jnp.zeros((fluid_count * capacity, span_dev), jnp.float32).at[...]
    gather x2 -> x0, local copies, waits for them, and re-layouts: 4.48 us -> none  [the longest x1 2.91 us: body(): lookup = extended[slot_index].reshape(fluid_count, capacity, span_dev)]
  transfers between devices with their start and end apart: 6 -> 0, of which waited for: 5 -> 0; matrix products, arithmetic and copies ran while one was open for 7% -> 0% of each run, Pallas kernels for 0% -> 0%
where the time goes in v1:
time: 48.5 us; the launch traced here: 48.1 us
  Pallas kernels  36.8 us (76%)
  local copies, waits for them, and re-layouts  10.7 us (22%)
  between operations  0.66 us (1%)
    pallas_call x1, Pallas kernels, body(): pl.pallas_call(functools.partial(kernel, fluids, metals, cap), out_shape=...  36.8 us
    unnamed x21, local copies, waits for them, and re-layouts  10.7 us

profile of v1, /device:TPU:0, one launch (start us, length us, event | category | flops | bytes accessed | tf_op | source)
XLA Modules:
  0.0 48.1 jit_solution(4710880253689112890)
XLA Ops:
  0.6 0.0 copy-start
  0.6 1.6 %copy-done = bf16[4,8,128,256]{3,2,1,0:T(8,128)(2,1)S(1)} copy-done((bf16[4,8,128,256]{3,2,1,0:T(8,128)(2,1)S(1)}, bf16[4,8,128,256]{3,2,1,0:T(8,128)(2,1)}, u32[]{:S(2)}) %copy-start) | copy-done | bytes 2097176
  2.2 0.0 copy-start.1
  2.2 1.2 %copy-done.1 = bf16[1,512,1024]{2,1,0:T(8,128)(2,1)S(1)} copy-done((bf16[1,512,1024]{2,1,0:T(8,128)(2,1)S(1)}, bf16[1,512,1024]{2,1,0:T(8,128)(2,1)}, u32[]{:S(2)}) %copy-start.1) | copy-done | bytes 1048600
  3.5 0.0 copy-start.2
  3.5 1.0 %copy-done.2 = f32[4,128,256]{2,1,0:T(8,128)S(1)} copy-done((f32[4,128,256]{2,1,0:T(8,128)S(1)}, f32[4,128,256]{2,1,0:T(8,128)}, u32[]{:S(2)}) %copy-start.2) | copy-done | bytes 524312
  4.5 0.0 copy-start.3
  4.5 1.0 %copy-done.3 = f32[1,512,256]{2,1,0:T(8,128)S(1)} copy-done((f32[1,512,256]{2,1,0:T(8,128)S(1)}, f32[1,512,256]{2,1,0:T(8,128)}, u32[]{:S(2)}) %copy-start.3) | copy-done | bytes 524312
  5.5 0.0 copy-start.4
  5.5 0.7 %copy-done.4 = f32[4,128]{1,0:T(4,128)S(1)} copy-done((f32[4,128]{1,0:T(4,128)S(1)}, f32[4,128]{1,0:T(4,128)}, u32[]{:S(2)}) %copy-start.4) | copy-done | bytes 2072
  6.2 0.0 copy-start.5
  6.2 0.7 %copy-done.5 = s32[4,128,1]{1,2,0:T(1,128)S(1)} copy-done((s32[4,128,1]{1,2,0:T(1,128)S(1)}, s32[4,128,1]{1,2,0:T(1,128)}, u32[]{:S(2)}) %copy-start.5) | copy-done | bytes 2072
  6.9 0.0 copy-start.6
  6.9 0.7 %copy-done.6 = s32[4,128]{1,0:T(4,128)S(1)} copy-done((s32[4,128]{1,0:T(4,128)S(1)}, s32[4,128]{1,0:T(4,128)}, u32[]{:S(2)}) %copy-start.6) | copy-done | bytes 2072
  7.6 0.0 copy-start.7
  7.6 0.7 %copy-done.7 = f32[1,512]{1,0:T(1,128)S(1)} copy-done((f32[1,512]{1,0:T(1,128)S(1)}, f32[1,512]{1,0:T(1,128)}, u32[]{:S(2)}) %copy-start.7) | copy-done | bytes 2072
  8.3 0.0 copy-start.8
  8.3 0.7 %copy-done.8 = s32[4]{0:T(128)S(1)} copy-done((s32[4]{0:T(128)S(1)}, s32[4]{0:T(128)}, u32[]{:S(2)}) %copy-start.8) | copy-done | bytes 40
  8.9 36.8 %shard_map.112 = (f32[512,256]{1,0:T(8,128)S(1)}, f32[512,256]{1,0:T(8,128)S(1)}, f32[512,256]{1,0:T(8,128)S(1)}) custom-call(s32[4]{0:T(128)S(1)} %copy-done.8, bf16[4,8,128,256]{3,2,1,0:T(8,128)(2,1)S(1)} %copy-done, f32[512,256]{1,0:T(8,128)S(1)} %bitcast.8, f32[4,128]{1,0:T(4,128)S(1)} %copy-done.4, s32[4,128]{1,0:T(4,128)S(1)} %bitcast.13, ...), custom_call_target="tpu_custom_call" | custom-call | tf_op jit(solution)/shard_map/pallas_call | solution.py:322
  45.7 0.8 %copy.15 = f32[1,512,256]{2,1,0:T(8,128)} copy(f32[1,512,256]{2,1,0:T(8,128)S(1)} %bitcast.12) | data formatting | bytes 1048576
  46.5 0.8 %copy.16 = f32[1,512,256]{2,1,0:T(8,128)} copy(f32[1,512,256]{2,1,0:T(8,128)S(1)} %bitcast.11) | data formatting | bytes 1048576
  47.3 0.8 %copy.17 = f32[4,128,256]{2,1,0:T(8,128)} copy(f32[4,128,256]{2,1,0:T(8,128)S(1)} %bitcast.10) | data formatting | bytes 1048576
Async XLA Ops:
  0.6 1.6 %copy-start = (bf16[4,8,128,256]{3,2,1,0:T(8,128)(2,1)S(1)}, bf16[4,8,128,256]{3,2,1,0:T(8,128)(2,1)}, u32[]{:S(2)}) copy-start(bf16[4,8,128,256]{3,2,1,0:T(8,128)(2,1)} %fluid_in.1) | copy-start | bytes 6291460
  2.2 1.2 %copy-start.1 = (bf16[1,512,1024]{2,1,0:T(8,128)(2,1)S(1)}, bf16[1,512,1024]{2,1,0:T(8,128)(2,1)}, u32[]{:S(2)}) copy-start(bf16[1,512,1024]{2,1,0:T(8,128)(2,1)} %param.15) | copy-start | bytes 3145732
  3.5 1.0 %copy-start.2 = (f32[4,128,256]{2,1,0:T(8,128)S(1)}, f32[4,128,256]{2,1,0:T(8,128)}, u32[]{:S(2)}) copy-start(f32[4,128,256]{2,1,0:T(8,128)} %param.10) | copy-start | bytes 1572868
  4.5 1.0 %copy-start.3 = (f32[1,512,256]{2,1,0:T(8,128)S(1)}, f32[1,512,256]{2,1,0:T(8,128)}, u32[]{:S(2)}) copy-start(f32[1,512,256]{2,1,0:T(8,128)} %param.17) | copy-start | bytes 1572868
  5.5 0.7 %copy-start.4 = (f32[4,128]{1,0:T(4,128)S(1)}, f32[4,128]{1,0:T(4,128)}, u32[]{:S(2)}) copy-start(f32[4,128]{1,0:T(4,128)} %cond.1) | copy-start | bytes 6148
  6.2 0.7 %copy-start.5 = (s32[4,128,1]{1,2,0:T(1,128)S(1)}, s32[4,128,1]{1,2,0:T(1,128)}, u32[]{:S(2)}) copy-start(s32[4,128,1]{1,2,0:T(1,128)} %param.13) | copy-start | bytes 6148
  6.9 0.7 %copy-start.6 = (s32[4,128]{1,0:T(4,128)S(1)}, s32[4,128]{1,0:T(4,128)}, u32[]{:S(2)}) copy-start(s32[4,128]{1,0:T(4,128)} %slot.1) | copy-start | bytes 6148
  7.6 0.7 %copy-start.7 = (f32[1,512]{1,0:T(1,128)S(1)}, f32[1,512]{1,0:T(1,128)}, u32[]{:S(2)}) copy-start(f32[1,512]{1,0:T(1,128)} %cool.1) | copy-start | bytes 6148
  8.3 0.7 %copy-start.8 = (s32[4]{0:T(128)S(1)}, s32[4]{0:T(128)}, u32[]{:S(2)}) copy-start(s32[4]{0:T(128)} %valid.1) | copy-start | bytes 52

commit v2 on v1

--- a/solution.py
+++ b/solution.py
@@ -11,6 +11,7 @@
 span_mix = 0.25
 relaxation = 0.5
 code_limit = 32512.0
+vmem_grant = 56 * 1024 * 1024
 MESH = pl.DeviceIdType.MESH
 f32, bf16, i32, i16 = jnp.float32, jnp.bfloat16, jnp.int32, jnp.int16
 
@@ -83,13 +84,13 @@
 
 def kernel(
     fluids, metals, cap,
-    valid, fluid_in, wall_in, cond, owner, slot, resp_in, cool, old_in,
+    valid_in, fluid_in, wall_in, cond_in, owner_in, slot_in, resp_in, cool_in, old_in,
     favg_out, mwall_out, wnew_out,
-    fluid_v, wall_v, resp_v, old_v,
+    favg_v, mwall_v, wnew_v, face_v, halo_f, wall_v, valid,
+    cond, owner, slot, cool, fluid_v, resp_v, old_v,
     pack, unpack, spread, fetch,
     meta_s, meta_r, flux_s, flux_r, fstep_s, fstep_r,
-    low_v, temp_v, halo_t, back_s, back_r, bstep_s, bstep_r, face_v, halo_f,
-    favg_v, mwall_v, wnew_v,
+    low_v, temp_v, halo_t, back_s, back_r, bstep_s, bstep_r,
     local_sem, meta_sem, flux_sem, fstep_sem, low_sem, halo_sem, back_sem, bstep_sem,
 ):
     blocks, layers, cells, span_dev = fluid_v.shape
@@ -105,7 +106,11 @@
     loads = [
         pltpu.make_async_copy(src, dst, local_sem.at[i])
         for i, (src, dst) in enumerate(
-            ((fluid_in, fluid_v), (wall_in, wall_v), (old_in, old_v), (resp_in, resp_v))
+            (
+                (valid_in, valid), (owner_in, owner), (slot_in, slot), (fluid_in, fluid_v),
+                (cond_in, cond), (wall_in, wall_v), (cool_in, cool), (old_in, old_v),
+                (resp_in, resp_v),
+            )
         )
     ]
     for load in loads:
@@ -124,10 +129,13 @@
             device_id=where, device_id_type=MESH,
         )
 
+    for load in loads[:3]:
+        load.wait()
+
     away = jnp.concatenate([owner[b : b + 1, :] for b in range(blocks)], axis=1) - me_f
     away = jnp.where(away < 0, away + fluids, away)
     cell = lax.broadcasted_iota(i32, (1, cells), 1)
-    live = jnp.concatenate([(cell < valid[b]).astype(i32) for b in range(blocks)], axis=1)
+    live = jnp.concatenate([(cell < valid[0:1, b : b + 1]).astype(i32) for b in range(blocks)], axis=1)
     away = jnp.where(live > 0, away, -1)
     lines = -(-fluids // 16) * 16
     chosen = lax.broadcasted_iota(i32, (lines, rows), 0) == away
@@ -164,8 +172,8 @@
         for r in range(1, fluids)
     ]
 
-    loads[0].wait()
-    loads[1].wait()
+    for load in loads[3:6]:
+        load.wait()
     weights = [2.0 * (layers - l) / (layers * (layers + 1.0)) for l in range(layers)]
     flux = []
     for b in range(blocks):
@@ -173,7 +181,7 @@
         for l in range(1, layers):
             near = near + weights[l] * fluid_v[b, l].astype(f32)
         gain = to_column(cond[b : b + 1, :])
-        lives = lax.broadcasted_iota(i32, (cells, 1), 0) < valid[b]
+        lives = lax.broadcasted_iota(i32, (cells, 1), 0) < valid[0:1, b : b + 1]
         flux.append(
             jnp.where(lives, gain * (near - wall_v[b * cells : (b + 1) * cells, :]), 0.0)
         )
@@ -211,9 +219,9 @@
     fetch[...] = (
         lax.broadcasted_iota(i32, (total, slots), 1).astype(f32) == to_column(arrived)
     ).astype(f32).astype(bf16)
+    for load in loads[6:]:
+        load.wait()
     cool_col = to_column(cool[...])
-    loads[2].wait()
-    loads[3].wait()
 
     averages, backs, bsteps = [], [], []
     for c in range(2):
@@ -237,8 +245,8 @@
         ]
         if c == 1:
             favg_v[...] = unpick(*averages)
-            store_favg = pltpu.make_async_copy(favg_v, favg_out, local_sem.at[4])
-            store_favg.start()
+            stores = [pltpu.make_async_copy(favg_v, favg_out, local_sem.at[9])]
+            stores[0].start()
         temp = cool_col
         for r in range(metals):
             if r:
@@ -270,8 +278,8 @@
 
     edge_t.wait_recv()
     mwall_v[...] = smooth(temp_v[0], temp_v[1], halo_t[...])
-    store_mwall = pltpu.make_async_copy(mwall_v, mwall_out, local_sem.at[5])
-    store_mwall.start()
+    stores.append(pltpu.make_async_copy(mwall_v, mwall_out, local_sem.at[10]))
+    stores[1].start()
 
     for c in range(2):
         for copy in bsteps[c] + backs[c]:
@@ -288,20 +296,34 @@
         if c == 0:
             edge_f = send(remote(face_v.at[0], halo_f, halo_sem, (1,), {"span": mate}))
     edge_f.wait_recv()
-    face = smooth(face_v[0], face_v[1], halo_f[...])
     for b in range(blocks):
-        lives = lax.broadcasted_iota(i32, (cells, 1), 0) < valid[b]
-        part = slice(b * cells, (b + 1) * cells)
+        lives = lax.broadcasted_iota(i32, (cells, 1), 0) < valid[0:1, b : b + 1]
+        part = pl.ds(b * cells, cells)
+        face = smooth(face_v[0, part, :], face_v[1, part, :], halo_f[part, :])
         wnew_v[part, :] = jnp.where(
-            lives, (1.0 - relaxation) * wall_v[part, :] + relaxation * face[part], 0.0
-        )
-    store_wnew = pltpu.make_async_copy(wnew_v, wnew_out, local_sem.at[6])
-    store_wnew.start()
+            lives, (1.0 - relaxation) * wall_v[part, :] + relaxation * face, 0.0
+        )
+        store = pltpu.make_async_copy(
+            wnew_v.at[part, :], wnew_out.at[part, :], local_sem.at[11 + b]
+        )
+        store.start()
+        stores.append(store)
     for copy in sends:
         copy.wait_send()
-    store_favg.wait()
-    store_mwall.wait()
-    store_wnew.wait()
+    for store in stores:
+        store.wait()
+
+
+def hand_over(*refs):
+    count = (len(refs) - 1) // 2
+    sem = refs[-1]
+    copies = [
+        pltpu.make_async_copy(refs[i], refs[count + i], sem.at[i]) for i in range(count)
+    ]
+    for copy in copies:
+        copy.start()
+    for copy in copies:
+        copy.wait()
 
 
 def body(
@@ -315,22 +337,30 @@
     slots = response.shape[1]
     width = span_dev // 2
     total = fluids * cap
-    vmem = pl.BlockSpec(memory_space=pltpu.VMEM)
-    smem = pl.BlockSpec(memory_space=pltpu.SMEM)
-    anywhere = pl.BlockSpec(memory_space=pl.ANY)
+    hbm = pl.BlockSpec(memory_space=pltpu.HBM)
     dma = pltpu.SemaphoreType.DMA
-    out = pl.pallas_call(
+    held = pl.pallas_call(
         functools.partial(kernel, fluids, metals, cap),
         out_shape=[
             jax.ShapeDtypeStruct((slots, span_dev), f32),
             jax.ShapeDtypeStruct((slots, span_dev), f32),
             jax.ShapeDtypeStruct((rows, span_dev), f32),
         ],
-        in_specs=[smem, anywhere, anywhere, vmem, vmem, vmem, anywhere, vmem, anywhere],
-        out_specs=[anywhere] * 3,
+        in_specs=[hbm] * 9,
+        out_specs=[hbm] * 3,
         scratch_shapes=[
+            pltpu.VMEM((slots, span_dev), f32),
+            pltpu.VMEM((slots, span_dev), f32),
+            pltpu.VMEM((rows, span_dev), f32),
+            pltpu.VMEM((2, rows, width), f32),
+            pltpu.VMEM((rows, width), f32),
+            pltpu.VMEM((rows, span_dev), f32),
+            pltpu.VMEM((1, blocks), i32),
+            pltpu.VMEM((blocks, cells), f32),
+            pltpu.VMEM((blocks, cells), i32),
+            pltpu.VMEM((blocks, cells), i32),
+            pltpu.VMEM((1, slots), f32),
             pltpu.VMEM(fluid_temp.shape, bf16),
-            pltpu.VMEM((rows, span_dev), f32),
             pltpu.VMEM(response.shape[1:], bf16),
             pltpu.VMEM((slots, span_dev), f32),
             pltpu.VMEM((total, rows), bf16),
@@ -350,12 +380,7 @@
             pltpu.VMEM((2, fluids, cap, width), i16),
             pltpu.VMEM((2, 8, 128), f32),
             pltpu.VMEM((2, fluids, 8, 128), f32),
-            pltpu.VMEM((2, rows, width), f32),
-            pltpu.VMEM((rows, width), f32),
-            pltpu.VMEM((slots, span_dev), f32),
-            pltpu.VMEM((slots, span_dev), f32),
-            pltpu.VMEM((rows, span_dev), f32),
-            dma((7,)),
+            dma((11 + blocks,)),
             dma((2, fluids)),
             dma((2, 2, fluids)),
             dma((2, 2, fluids)),
@@ -365,10 +390,10 @@
             dma((2, 2, fluids)),
         ],
         compiler_params=pltpu.CompilerParams(
-            collective_id=0, has_side_effects=True, vmem_limit_bytes=48 * 1024 * 1024
+            collective_id=0, has_side_effects=True, vmem_limit_bytes=vmem_grant
         ),
     )(
-        valid_rows,
+        valid_rows.reshape(1, blocks),
         fluid_temp,
         wall_old.reshape(rows, span_dev),
         conductance,
@@ -378,6 +403,14 @@
         coolant,
         flux_old[0],
     )
+    out = pl.pallas_call(
+        hand_over,
+        out_shape=[jax.ShapeDtypeStruct(x.shape, x.dtype) for x in held],
+        in_specs=[hbm] * 3,
+        out_specs=[hbm] * 3,
+        scratch_shapes=[dma((3,))],
+        compiler_params=pltpu.CompilerParams(vmem_limit_bytes=vmem_grant),
+    )(*held)
     return out[0][None], out[1][None], out[2].reshape(blocks, cells, span_dev)
 
 

time: 48.5 us -> 86.5 us (1.78)
  Pallas kernels: 36.8 us -> 85.7 us
  local copies, waits for them, and re-layouts: 10.7 us -> 0 us
    pallas_call x0 -> x1, Pallas kernels: none -> 48.8 us  [body(): pl.pallas_call(hand_over, out_shape=[jax.ShapeDtypeStruct(x.shape, x.dtyp...]
    unnamed x21 -> x0, local copies, waits for them, and re-layouts: 10.7 us -> none
where the time goes in v2:
time: 86.5 us; the launch traced here: 86.4 us
  Pallas kernels  85.7 us (99%)
    pallas_call x1, Pallas kernels, body(): pl.pallas_call(hand_over, out_shape=[jax.ShapeDtypeStruct(x.shape, x.dtyp...  48.8 us
    pallas_call x1, Pallas kernels, body(): pl.pallas_call(functools.partial(kernel, fluids, metals, cap), out_shape=...  37 us

profile of v2, /device:TPU:0, one launch (start us, length us, event | category | flops | bytes accessed | tf_op | source)
XLA Modules:
  0.0 86.4 jit_solution(5263205277802745765)
XLA Ops:
  0.6 37.0 %shard_map.112 = (f32[512,256]{1,0:T(8,128)}, f32[512,256]{1,0:T(8,128)}, f32[512,256]{1,0:T(8,128)}) custom-call(s32[1,4]{1,0:T(1,128)} %bitcast.12, bf16[4,8,128,256]{3,2,1,0:T(8,128)(2,1)} %fluid_in.1, f32[512,256]{1,0:T(8,128)} %bitcast.9, f32[4,128]{1,0:T(4,128)} %cond_in.1, s32[4,128]{1,0:T(4,128)} %bitcast.11, s32[4,128]{1,0:T(4,128)} %slot_in.1, ...), custom_call_target="tpu_custom_call" | custom-call | tf_op jit(solution)/shard_map/pallas_call | solution.py:342
  37.6 48.8 %shard_map.113 = (f32[512,256]{1,0:T(8,128)}, f32[512,256]{1,0:T(8,128)}, f32[512,256]{1,0:T(8,128)}) custom-call(f32[512,256]{1,0:T(8,128)} %get-tuple-element.9.refs_0_, f32[512,256]{1,0:T(8,128)} %get-tuple-element.10.refs_1_, f32[512,256]{1,0:T(8,128)} %get-tuple-element.11.refs_2_), custom_call_target="tpu_custom_call" | custom-call | tf_op jit(solution)/shard_map/pallas_call | solution.py:406

commit v3 on v2

--- a/solution.py
+++ b/solution.py
@@ -12,6 +12,7 @@
 relaxation = 0.5
 code_limit = 32512.0
 vmem_grant = 56 * 1024 * 1024
+ln2 = 0.6931471805599453
 MESH = pl.DeviceIdType.MESH
 f32, bf16, i32, i16 = jnp.float32, jnp.bfloat16, jnp.int32, jnp.int16
 
@@ -33,8 +34,29 @@
 
 def encode(x):
     top = jnp.maximum(jnp.max(jnp.abs(x), keepdims=True), 1e-30)
-    code = jnp.floor(x * (code_limit / top) + 0.5)
-    return code, top * (1.0 / code_limit)
+    level = jnp.floor(jnp.log(top) * (16.0 / ln2)) + 2.0
+    return jnp.floor(x * (code_limit * jnp.exp(level * (-ln2 / 16.0))) + 0.5), level
+
+
+def decode(block, cap):
+    level = block[cap:].astype(i32).astype(f32)[0:1]
+    return block[:cap].astype(i32).astype(f32) * (jnp.exp(level * (ln2 / 16.0)) * (1.0 / code_limit))
+
+
+def fill(here, away, chunk, codes, level, cap):
+    codes = codes.astype(i32).astype(i16)
+    mark = jnp.broadcast_to(level, (16, codes.shape[1])).astype(i32).astype(i16)
+    for r in range(codes.shape[0] // cap):
+        dst = away if r else here
+        dst[chunk, r, 0:cap] = codes[r * cap : (r + 1) * cap]
+        dst[chunk, r, cap : cap + 16] = mark
+
+
+def partner(me, r):
+    for bit in range(r.bit_length()):
+        if (r >> bit) & 1:
+            me = me + (1 << bit) * (1 - 2 * ((me // (1 << bit)) % 2))
+    return me
 
 
 def code_parts(code):
@@ -89,17 +111,17 @@
     favg_v, mwall_v, wnew_v, face_v, halo_f, wall_v, valid,
     cond, owner, slot, cool, fluid_v, resp_v, old_v,
     pack, unpack, spread, fetch,
-    meta_s, meta_r, flux_s, flux_r, fstep_s, fstep_r,
-    low_v, temp_v, halo_t, back_s, back_r, bstep_s, bstep_r,
-    local_sem, meta_sem, flux_sem, fstep_sem, low_sem, halo_sem, back_sem, bstep_sem,
+    meta_s, meta_r, flux_s, flux_r,
+    low_v, temp_v, halo_t, back_s, back_r,
+    local_sem, meta_sem, flux_sem, low_sem, halo_sem, back_sem,
 ):
     blocks, layers, cells, span_dev = fluid_v.shape
     rows = blocks * cells
     slots = resp_v.shape[0]
     width = span_dev // 2
     me_f, me_m, me_s = lax.axis_index("fluid"), lax.axis_index("metal"), lax.axis_index("span")
-    up = [None] + [lax.rem(me_f + r, fluids) for r in range(1, fluids)]
-    down = [None] + [lax.rem(me_f + fluids - r, fluids) for r in range(1, fluids)]
+    peers = [partner(me_f, r) for r in range(fluids)]
+    order = list(range(fluids - 1, 0, -1))
     across = [None] + [lax.rem(me_m + r, metals) for r in range(1, metals)]
     mate = 1 - me_s
 
@@ -117,8 +139,8 @@
         load.start()
 
     barrier = pltpu.get_barrier_semaphore()
-    for r in range(1, fluids):
-        pl.semaphore_signal(barrier, inc=1, device_id={"fluid": up[r]}, device_id_type=MESH)
+    for r in order:
+        pl.semaphore_signal(barrier, inc=1, device_id={"fluid": peers[r]}, device_id_type=MESH)
     for r in range(1, metals):
         pl.semaphore_signal(barrier, inc=1, device_id={"metal": across[r]}, device_id_type=MESH)
     pl.semaphore_signal(barrier, inc=1, device_id={"span": mate}, device_id_type=MESH)
@@ -132,8 +154,7 @@
     for load in loads[:3]:
         load.wait()
 
-    away = jnp.concatenate([owner[b : b + 1, :] for b in range(blocks)], axis=1) - me_f
-    away = jnp.where(away < 0, away + fluids, away)
+    away = jnp.concatenate([owner[b : b + 1, :] for b in range(blocks)], axis=1) ^ me_f
     cell = lax.broadcasted_iota(i32, (1, cells), 1)
     live = jnp.concatenate([(cell < valid[0:1, b : b + 1]).astype(i32) for b in range(blocks)], axis=1)
     away = jnp.where(live > 0, away, -1)
@@ -147,14 +168,13 @@
     pack[...] = (
         lax.broadcasted_iota(i32, (total, rows), 0).astype(f32) == place
     ).astype(f32).astype(bf16)
-    place_col = to_column(place)
-    unpack[...] = (
-        lax.broadcasted_iota(i32, (rows, total), 1).astype(f32) == place_col
-    ).astype(f32).astype(bf16)
     slot_row = jnp.concatenate([slot[b : b + 1, :] for b in range(blocks)], axis=1)
     line = lax.broadcasted_iota(i32, (16, rows), 0)
     halves = jnp.where(line == 0, slot_row // 256, jnp.where(line == 1, slot_row % 256, 0))
-    packed_slots = mm(halves.astype(f32).astype(bf16), unpack[...])
+    packed_slots = lax.dot_general(
+        halves.astype(f32).astype(bf16), pack[...], (((1,), (1,)), ((), ())),
+        preferred_element_type=f32,
+    )
     packed_slots = 256.0 * packed_slots[0:1] + packed_slots[1:2]
     for r in range(fluids):
         meta_s[r, :, 0:cap] = jnp.broadcast_to(packed_slots[:, r * cap : (r + 1) * cap], (8, cap))
@@ -168,8 +188,8 @@
         return copy
 
     metas = [
-        send(remote(meta_s.at[r], meta_r.at[r], meta_sem, (r,), {"fluid": up[r]}))
-        for r in range(1, fluids)
+        send(remote(meta_s.at[r], meta_r.at[r], meta_sem, (r,), {"fluid": peers[r]}))
+        for r in order
     ]
 
     for load in loads[3:6]:
@@ -187,26 +207,19 @@
         )
     flux = jnp.concatenate(flux, axis=0)
 
-    fluxes, fsteps = [], []
+    fluxes = []
     for c in range(2):
-        code, step = encode(pick(flux, c))
-        fstep_s[c] = jnp.broadcast_to(step, (8, 128))
-        packed = from_parts(mm(pack[...], code_parts(code))).astype(i32).astype(i16)
-        for r in range(fluids):
-            dst = flux_r if r == 0 else flux_s
-            dst[c, r] = packed[r * cap : (r + 1) * cap]
-        fsteps.append(
-            [
-                send(remote(fstep_s.at[c], fstep_r.at[c, r], fstep_sem, (c, r), {"fluid": up[r]}))
-                for r in range(1, fluids)
-            ]
-        )
+        code, level = encode(pick(flux, c))
+        fill(flux_r, flux_s, c, from_parts(mm(pack[...], code_parts(code))), level, cap)
         fluxes.append(
             [
-                send(remote(flux_s.at[c, r], flux_r.at[c, r], flux_sem, (c, r), {"fluid": up[r]}))
-                for r in range(1, fluids)
+                send(remote(flux_s.at[c, r], flux_r.at[c, r], flux_sem, (c, r), {"fluid": peers[r]}))
+                for r in order
             ]
         )
+    unpack[...] = (
+        lax.broadcasted_iota(i32, (rows, total), 1).astype(f32) == to_column(place)
+    ).astype(f32).astype(bf16)
 
     for copy in metas:
         copy.wait_recv()
@@ -223,17 +236,12 @@
         load.wait()
     cool_col = to_column(cool[...])
 
-    averages, backs, bsteps = [], [], []
+    averages, backs = [], []
     for c in range(2):
-        for copy in fsteps[c] + fluxes[c]:
+        for copy in fluxes[c]:
             copy.wait_recv()
         incoming = jnp.concatenate(
-            [
-                flux_r[c, r].astype(i32).astype(f32)
-                * (fstep_s[c, 0:1, :] if r == 0 else fstep_r[c, r, 0:1, :])
-                for r in range(fluids)
-            ],
-            axis=0,
+            [decode(flux_r[c, r], cap) for r in range(fluids)], axis=0
         )
         summed = add_parts(mm(spread[...], value_parts(incoming)))
         average = (1.0 - average_weight) * pick(old_v[...], c) + average_weight * summed
@@ -257,22 +265,12 @@
         temp_v[c] = temp
         if c == 0:
             edge_t = send(remote(temp_v.at[0], halo_t, halo_sem, (0,), {"span": mate}))
-        code, step = encode(temp)
-        bstep_s[c] = jnp.broadcast_to(step, (8, 128))
-        found = from_parts(mm(fetch[...], code_parts(code))).astype(i32).astype(i16)
-        for r in range(fluids):
-            dst = back_r if r == 0 else back_s
-            dst[c, r] = found[r * cap : (r + 1) * cap]
-        bsteps.append(
-            [
-                send(remote(bstep_s.at[c], bstep_r.at[c, r], bstep_sem, (c, r), {"fluid": down[r]}))
-                for r in range(1, fluids)
-            ]
-        )
+        code, level = encode(temp)
+        fill(back_r, back_s, c, from_parts(mm(fetch[...], code_parts(code))), level, cap)
         backs.append(
             [
-                send(remote(back_s.at[c, r], back_r.at[c, r], back_sem, (c, r), {"fluid": down[r]}))
-                for r in range(1, fluids)
+                send(remote(back_s.at[c, r], back_r.at[c, r], back_sem, (c, r), {"fluid": peers[r]}))
+                for r in order
             ]
         )
 
@@ -282,15 +280,10 @@
     stores[1].start()
 
     for c in range(2):
-        for copy in bsteps[c] + backs[c]:
+        for copy in backs[c]:
             copy.wait_recv()
         returned = jnp.concatenate(
-            [
-                back_r[c, r].astype(i32).astype(f32)
-                * (bstep_s[c, 0:1, :] if r == 0 else bstep_r[c, r, 0:1, :])
-                for r in range(fluids)
-            ],
-            axis=0,
+            [decode(back_r[c, r], cap) for r in range(fluids)], axis=0
         )
         face_v[c] = add_parts(mm(unpack[...], value_parts(returned)))
         if c == 0:
@@ -315,15 +308,19 @@
 
 
 def hand_over(*refs):
-    count = (len(refs) - 1) // 2
-    sem = refs[-1]
-    copies = [
-        pltpu.make_async_copy(refs[i], refs[count + i], sem.at[i]) for i in range(count)
-    ]
-    for copy in copies:
-        copy.start()
-    for copy in copies:
-        copy.wait()
+    count = (len(refs) - 2) // 3
+    sources, targets, held, (load_sem, store_sem) = (
+        refs[:count], refs[count : 2 * count], refs[2 * count : 3 * count], refs[3 * count :]
+    )
+    loads = [pltpu.make_async_copy(sources[i], held[i], load_sem.at[i]) for i in range(count)]
+    stores = [pltpu.make_async_copy(held[i], targets[i], store_sem.at[i]) for i in range(count)]
+    for load in loads:
+        load.start()
+    for load, store in zip(loads, stores):
+        load.wait()
+        store.start()
+    for store in stores:
+        store.wait()
 
 
 def body(
@@ -369,24 +366,18 @@
             pltpu.VMEM((total, slots), bf16),
             pltpu.VMEM((fluids, 8, lanes), f32),
             pltpu.VMEM((fluids, 8, lanes), f32),
-            pltpu.VMEM((2, fluids, cap, width), i16),
-            pltpu.VMEM((2, fluids, cap, width), i16),
-            pltpu.VMEM((2, 8, 128), f32),
-            pltpu.VMEM((2, fluids, 8, 128), f32),
+            pltpu.VMEM((2, fluids, cap + 16, width), i16),
+            pltpu.VMEM((2, fluids, cap + 16, width), i16),
             pltpu.VMEM((2, metals, slots, width), bf16),
             pltpu.VMEM((2, slots, width), f32),
             pltpu.VMEM((slots, width), f32),
-            pltpu.VMEM((2, fluids, cap, width), i16),
-            pltpu.VMEM((2, fluids, cap, width), i16),
-            pltpu.VMEM((2, 8, 128), f32),
-            pltpu.VMEM((2, fluids, 8, 128), f32),
+            pltpu.VMEM((2, fluids, cap + 16, width), i16),
+            pltpu.VMEM((2, fluids, cap + 16, width), i16),
             dma((11 + blocks,)),
             dma((2, fluids)),
             dma((2, 2, fluids)),
-            dma((2, 2, fluids)),
             dma((2, 2, metals)),
             dma((2, 2)),
-            dma((2, 2, fluids)),
             dma((2, 2, fluids)),
         ],
         compiler_params=pltpu.CompilerParams(
@@ -408,7 +399,7 @@
         out_shape=[jax.ShapeDtypeStruct(x.shape, x.dtype) for x in held],
         in_specs=[hbm] * 3,
         out_specs=[hbm] * 3,
-        scratch_shapes=[dma((3,))],
+        scratch_shapes=[pltpu.VMEM(x.shape, x.dtype) for x in held] + [dma((3,)), dma((3,))],
         compiler_params=pltpu.CompilerParams(vmem_limit_bytes=vmem_grant),
     )(*held)
     return out[0][None], out[1][None], out[2].reshape(blocks, cells, span_dev)

time: 86.5 us -> 37.2 us (0.43)
  Pallas kernels: 85.7 us -> 36.4 us
    pallas_call x1, Pallas kernels: 48.8 us -> 2.23 us  [body(): pl.pallas_call(hand_over, out_shape=[jax.ShapeDtypeStruct(x.shape, x.dtyp...]
    pallas_call x1, Pallas kernels: 37 us -> 34.1 us  [body(): pl.pallas_call(functools.partial(kernel, fluids, metals, cap), out_shape=...]
where the time goes in v3:
time: 37.2 us; the launch traced here: 37 us
  Pallas kernels  36.4 us (98%)
  between operations  0.64 us (2%)
    pallas_call x1, Pallas kernels, body(): pl.pallas_call(functools.partial(kernel, fluids, metals, cap), out_shape=...  34.1 us
    pallas_call x1, Pallas kernels, body(): pl.pallas_call(hand_over, out_shape=[jax.ShapeDtypeStruct(x.shape, x.dtyp...  2.23 us

profile of v3, /device:TPU:0, one launch (start us, length us, event | category | flops | bytes accessed | tf_op | source)
XLA Modules:
  0.0 37.0 jit_solution(13833435051262209359)
XLA Ops:
  0.6 34.1 %shard_map.112 = (f32[512,256]{1,0:T(8,128)}, f32[512,256]{1,0:T(8,128)}, f32[512,256]{1,0:T(8,128)}) custom-call(s32[1,4]{1,0:T(1,128)} %bitcast.12, bf16[4,8,128,256]{3,2,1,0:T(8,128)(2,1)} %fluid_in.1, f32[512,256]{1,0:T(8,128)} %bitcast.9, f32[4,128]{1,0:T(4,128)} %cond_in.1, s32[4,128]{1,0:T(4,128)} %bitcast.11, s32[4,128]{1,0:T(4,128)} %slot_in.1, ...), custom_call_target="tpu_custom_call" | custom-call | tf_op jit(solution)/shard_map/pallas_call | solution.py:339
  34.8 2.2 %shard_map.113 = (f32[512,256]{1,0:T(8,128)}, f32[512,256]{1,0:T(8,128)}, f32[512,256]{1,0:T(8,128)}) custom-call(f32[512,256]{1,0:T(8,128)} %get-tuple-element.9.refs_0_, f32[512,256]{1,0:T(8,128)} %get-tuple-element.10.refs_1_, f32[512,256]{1,0:T(8,128)} %get-tuple-element.11.refs_2_), custom_call_target="tpu_custom_call" | custom-call | tf_op jit(solution)/shard_map/pallas_call | solution.py:397

commit v4 on v3

--- a/solution.py
+++ b/solution.py
@@ -38,18 +38,15 @@
     return jnp.floor(x * (code_limit * jnp.exp(level * (-ln2 / 16.0))) + 0.5), level
 
 
-def decode(block, cap):
-    level = block[cap:].astype(i32).astype(f32)[0:1]
-    return block[:cap].astype(i32).astype(f32) * (jnp.exp(level * (ln2 / 16.0)) * (1.0 / code_limit))
-
-
-def fill(here, away, chunk, codes, level, cap):
+def decode(codes, level):
+    return codes.astype(i32).astype(f32) * (jnp.exp(level * (ln2 / 16.0)) * (1.0 / code_limit))
+
+
+def fill(here, away, chunk, codes, cap):
     codes = codes.astype(i32).astype(i16)
-    mark = jnp.broadcast_to(level, (16, codes.shape[1])).astype(i32).astype(i16)
     for r in range(codes.shape[0] // cap):
         dst = away if r else here
-        dst[chunk, r, 0:cap] = codes[r * cap : (r + 1) * cap]
-        dst[chunk, r, cap : cap + 16] = mark
+        dst[chunk, r] = codes[r * cap : (r + 1) * cap]
 
 
 def partner(me, r):
@@ -112,8 +109,8 @@
     cond, owner, slot, cool, fluid_v, resp_v, old_v,
     pack, unpack, spread, fetch,
     meta_s, meta_r, flux_s, flux_r,
-    low_v, temp_v, halo_t, back_s, back_r,
-    local_sem, meta_sem, flux_sem, low_sem, halo_sem, back_sem,
+    low_v, temp_v, halo_t, back_s, back_r, blevel_s, blevel_r,
+    local_sem, meta_sem, flux_sem, low_sem, halo_sem, back_sem, blevel_sem,
 ):
     blocks, layers, cells, span_dev = fluid_v.shape
     rows = blocks * cells
@@ -129,13 +126,16 @@
         pltpu.make_async_copy(src, dst, local_sem.at[i])
         for i, (src, dst) in enumerate(
             (
-                (valid_in, valid), (owner_in, owner), (slot_in, slot), (fluid_in, fluid_v),
-                (cond_in, cond), (wall_in, wall_v), (cool_in, cool), (old_in, old_v),
-                (resp_in, resp_v),
+                (valid_in, valid), (owner_in, owner), (slot_in, slot), (cond_in, cond),
+                (wall_in, wall_v), (cool_in, cool), (old_in, old_v), (resp_in, resp_v),
             )
         )
     ]
-    for load in loads:
+    fluid_loads = [
+        pltpu.make_async_copy(fluid_in.at[b], fluid_v.at[b], local_sem.at[11 + blocks + b])
+        for b in range(blocks)
+    ]
+    for load in loads[:4] + fluid_loads + loads[4:5]:
         load.start()
 
     barrier = pltpu.get_barrier_semaphore()
@@ -176,27 +176,12 @@
         preferred_element_type=f32,
     )
     packed_slots = 256.0 * packed_slots[0:1] + packed_slots[1:2]
-    for r in range(fluids):
-        meta_s[r, :, 0:cap] = jnp.broadcast_to(packed_slots[:, r * cap : (r + 1) * cap], (8, cap))
-
-    pl.semaphore_wait(barrier, fluids + metals - 1)
-    sends = []
-
-    def send(copy):
-        copy.start()
-        sends.append(copy)
-        return copy
-
-    metas = [
-        send(remote(meta_s.at[r], meta_r.at[r], meta_sem, (r,), {"fluid": peers[r]}))
-        for r in order
-    ]
-
-    for load in loads[3:6]:
+    for load in loads[3:5]:
         load.wait()
     weights = [2.0 * (layers - l) / (layers * (layers + 1.0)) for l in range(layers)]
     flux = []
     for b in range(blocks):
+        fluid_loads[b].wait()
         near = weights[0] * fluid_v[b, 0].astype(f32)
         for l in range(1, layers):
             near = near + weights[l] * fluid_v[b, l].astype(f32)
@@ -206,11 +191,31 @@
             jnp.where(lives, gain * (near - wall_v[b * cells : (b + 1) * cells, :]), 0.0)
         )
     flux = jnp.concatenate(flux, axis=0)
+    for load in loads[5:]:
+        load.start()
+
+    flux, level = encode(flux)
+    lanes = meta_s.shape[2] - width
+    for r in range(fluids):
+        meta_s[r, :, 0:cap] = packed_slots[:, r * cap : (r + 1) * cap]
+        meta_s[r, :, lanes:] = jnp.broadcast_to(level, (1, width))
+
+    pl.semaphore_wait(barrier, fluids + metals - 1)
+    sends = []
+
+    def send(copy):
+        copy.start()
+        sends.append(copy)
+        return copy
+
+    metas = [
+        send(remote(meta_s.at[r], meta_r.at[r], meta_sem, (r,), {"fluid": peers[r]}))
+        for r in order
+    ]
 
     fluxes = []
     for c in range(2):
-        code, level = encode(pick(flux, c))
-        fill(flux_r, flux_s, c, from_parts(mm(pack[...], code_parts(code))), level, cap)
+        fill(flux_r, flux_s, c, from_parts(mm(pack[...], code_parts(pick(flux, c)))), cap)
         fluxes.append(
             [
                 send(remote(flux_s.at[c, r], flux_r.at[c, r], flux_sem, (c, r), {"fluid": peers[r]}))
@@ -224,7 +229,7 @@
     for copy in metas:
         copy.wait_recv()
     arrived = jnp.concatenate(
-        [packed_slots[:, 0:cap]] + [meta_r[r, 0:1, 0:cap] for r in range(1, fluids)], axis=1
+        [packed_slots[:, 0:cap]] + [meta_r[r, :, 0:cap] for r in range(1, fluids)], axis=1
     )
     spread[...] = (
         lax.broadcasted_iota(i32, (slots, total), 0).astype(f32) == arrived
@@ -232,33 +237,35 @@
     fetch[...] = (
         lax.broadcasted_iota(i32, (total, slots), 1).astype(f32) == to_column(arrived)
     ).astype(f32).astype(bf16)
-    for load in loads[6:]:
+    for load in loads[5:]:
         load.wait()
     cool_col = to_column(cool[...])
 
-    averages, backs = [], []
+    averages, lows, backs = [], [], []
     for c in range(2):
         for copy in fluxes[c]:
             copy.wait_recv()
         incoming = jnp.concatenate(
-            [decode(flux_r[c, r], cap) for r in range(fluids)], axis=0
+            [
+                decode(flux_r[c, r], (meta_r if r else meta_s)[r, :, lanes:])
+                for r in range(fluids)
+            ], axis=0
         )
         summed = add_parts(mm(spread[...], value_parts(incoming)))
         average = (1.0 - average_weight) * pick(old_v[...], c) + average_weight * summed
         averages.append(average)
         low_v[c, 0] = average.astype(bf16)
-        lows = [
-            send(remote(low_v.at[c, 0], low_v.at[c, r], low_sem, (c, r), {"metal": across[r]}))
-            for r in range(1, metals)
-        ]
-        if c == 1:
-            favg_v[...] = unpick(*averages)
-            stores = [pltpu.make_async_copy(favg_v, favg_out, local_sem.at[9])]
-            stores[0].start()
+        lows.append(
+            [
+                send(remote(low_v.at[c, 0], low_v.at[c, r], low_sem, (c, r), {"metal": across[r]}))
+                for r in range(1, metals)
+            ]
+        )
+    for c in range(2):
         temp = cool_col
         for r in range(metals):
             if r:
-                lows[r - 1].wait_recv()
+                lows[c][r - 1].wait_recv()
             stripe = lax.rem(me_m + metals - r, metals)
             columns = pl.ds(pl.multiple_of(stripe * slots, slots), slots)
             temp = temp + mm(resp_v[:, columns], low_v[c, r])
@@ -266,14 +273,22 @@
         if c == 0:
             edge_t = send(remote(temp_v.at[0], halo_t, halo_sem, (0,), {"span": mate}))
         code, level = encode(temp)
-        fill(back_r, back_s, c, from_parts(mm(fetch[...], code_parts(code))), level, cap)
+        blevel_s[c] = jnp.broadcast_to(level, (1, width))
+        fill(back_r, back_s, c, from_parts(mm(fetch[...], code_parts(code))), cap)
         backs.append(
             [
+                send(remote(blevel_s.at[c], blevel_r.at[c, r], blevel_sem, (c, r), {"fluid": peers[r]}))
+                for r in order
+            ]
+            + [
                 send(remote(back_s.at[c, r], back_r.at[c, r], back_sem, (c, r), {"fluid": peers[r]}))
                 for r in order
             ]
         )
 
+    favg_v[...] = unpick(*averages)
+    stores = [pltpu.make_async_copy(favg_v, favg_out, local_sem.at[9])]
+    stores[0].start()
     edge_t.wait_recv()
     mwall_v[...] = smooth(temp_v[0], temp_v[1], halo_t[...])
     stores.append(pltpu.make_async_copy(mwall_v, mwall_out, local_sem.at[10]))
@@ -283,7 +298,10 @@
         for copy in backs[c]:
             copy.wait_recv()
         returned = jnp.concatenate(
-            [decode(back_r[c, r], cap) for r in range(fluids)], axis=0
+            [
+                decode(back_r[c, r], blevel_r[c, r] if r else blevel_s[c])
+                for r in range(fluids)
+            ], axis=0
         )
         face_v[c] = add_parts(mm(unpack[...], value_parts(returned)))
         if c == 0:
@@ -364,20 +382,23 @@
             pltpu.VMEM((rows, total), bf16),
             pltpu.VMEM((slots, total), bf16),
             pltpu.VMEM((total, slots), bf16),
-            pltpu.VMEM((fluids, 8, lanes), f32),
-            pltpu.VMEM((fluids, 8, lanes), f32),
-            pltpu.VMEM((2, fluids, cap + 16, width), i16),
-            pltpu.VMEM((2, fluids, cap + 16, width), i16),
+            pltpu.VMEM((fluids, 1, lanes + width), f32),
+            pltpu.VMEM((fluids, 1, lanes + width), f32),
+            pltpu.VMEM((2, fluids, cap, width), i16),
+            pltpu.VMEM((2, fluids, cap, width), i16),
             pltpu.VMEM((2, metals, slots, width), bf16),
             pltpu.VMEM((2, slots, width), f32),
             pltpu.VMEM((slots, width), f32),
-            pltpu.VMEM((2, fluids, cap + 16, width), i16),
-            pltpu.VMEM((2, fluids, cap + 16, width), i16),
-            dma((11 + blocks,)),
+            pltpu.VMEM((2, fluids, cap, width), i16),
+            pltpu.VMEM((2, fluids, cap, width), i16),
+            pltpu.VMEM((2, 1, width), f32),
+            pltpu.VMEM((2, fluids, 1, width), f32),
+            dma((11 + 2 * blocks,)),
             dma((2, fluids)),
             dma((2, 2, fluids)),
             dma((2, 2, metals)),
             dma((2, 2)),
+            dma((2, 2, fluids)),
             dma((2, 2, fluids)),
         ],
         compiler_params=pltpu.CompilerParams(

time: 37.2 us -> 34.8 us (0.935)
  Pallas kernels: 36.4 us -> 33.9 us
    pallas_call x1, Pallas kernels: 34.1 us -> 31.7 us  [body(): pl.pallas_call(functools.partial(kernel, fluids, metals, cap), out_shape=...]
where the time goes in v4:
time: 34.8 us; the launch traced here: 34.6 us
  Pallas kernels  33.9 us (97%)
  between operations  0.64 us (2%)
    pallas_call x1, Pallas kernels, body(): pl.pallas_call(functools.partial(kernel, fluids, metals, cap), out_shape=...  31.7 us
    pallas_call x1, Pallas kernels, body(): pl.pallas_call(hand_over, out_shape=[jax.ShapeDtypeStruct(x.shape, x.dtyp...  2.23 us

profile of v4, /device:TPU:0, one launch (start us, length us, event | category | flops | bytes accessed | tf_op | source)
XLA Modules:
  0.0 34.6 jit_solution(6122608324610892129)
XLA Ops:
  0.6 31.7 %shard_map.112 = (f32[512,256]{1,0:T(8,128)}, f32[512,256]{1,0:T(8,128)}, f32[512,256]{1,0:T(8,128)}) custom-call(s32[1,4]{1,0:T(1,128)} %bitcast.12, bf16[4,8,128,256]{3,2,1,0:T(8,128)(2,1)} %fluid_in.1, f32[512,256]{1,0:T(8,128)} %bitcast.9, f32[4,128]{1,0:T(4,128)} %cond_in.1, s32[4,128]{1,0:T(4,128)} %bitcast.11, s32[4,128]{1,0:T(4,128)} %slot_in.1, ...), custom_call_target="tpu_custom_call" | custom-call | tf_op jit(solution)/shard_map/pallas_call | solution.py:357
  32.4 2.2 %shard_map.113 = (f32[512,256]{1,0:T(8,128)}, f32[512,256]{1,0:T(8,128)}, f32[512,256]{1,0:T(8,128)}) custom-call(f32[512,256]{1,0:T(8,128)} %get-tuple-element.9.refs_0_, f32[512,256]{1,0:T(8,128)} %get-tuple-element.10.refs_1_, f32[512,256]{1,0:T(8,128)} %get-tuple-element.11.refs_2_), custom_call_target="tpu_custom_call" | custom-call | tf_op jit(solution)/shard_map/pallas_call | solution.py:418

commit v5 on v4

--- a/solution.py
+++ b/solution.py
@@ -118,7 +118,7 @@
     width = span_dev // 2
     me_f, me_m, me_s = lax.axis_index("fluid"), lax.axis_index("metal"), lax.axis_index("span")
     peers = [partner(me_f, r) for r in range(fluids)]
-    order = list(range(fluids - 1, 0, -1))
+    order = list(range(2, fluids)) + [1]
     across = [None] + [lax.rem(me_m + r, metals) for r in range(1, metals)]
     mate = 1 - me_s
 

time: 34.8 us -> 34.1 us (0.980)
  Pallas kernels: 33.9 us -> 33.2 us
    pallas_call x1, Pallas kernels: 31.7 us -> 31 us  [body(): pl.pallas_call(functools.partial(kernel, fluids, metals, cap), out_shape=...]
where the time goes in v5:
time: 34.1 us; the launch traced here: 33.9 us
  Pallas kernels  33.2 us (97%)
  between operations  0.64 us (2%)
    pallas_call x1, Pallas kernels, body(): pl.pallas_call(functools.partial(kernel, fluids, metals, cap), out_shape=...  31 us
    pallas_call x1, Pallas kernels, body(): pl.pallas_call(hand_over, out_shape=[jax.ShapeDtypeStruct(x.shape, x.dtyp...  2.23 us

profile of v5, /device:TPU:0, one launch (start us, length us, event | category | flops | bytes accessed | tf_op | source)
XLA Modules:
  0.0 33.9 jit_solution(3377509329208974097)
XLA Ops:
  0.6 31.0 %shard_map.112 = (f32[512,256]{1,0:T(8,128)}, f32[512,256]{1,0:T(8,128)}, f32[512,256]{1,0:T(8,128)}) custom-call(s32[1,4]{1,0:T(1,128)} %bitcast.12, bf16[4,8,128,256]{3,2,1,0:T(8,128)(2,1)} %fluid_in.1, f32[512,256]{1,0:T(8,128)} %bitcast.9, f32[4,128]{1,0:T(4,128)} %cond_in.1, s32[4,128]{1,0:T(4,128)} %bitcast.11, s32[4,128]{1,0:T(4,128)} %slot_in.1, ...), custom_call_target="tpu_custom_call" | custom-call | tf_op jit(solution)/shard_map/pallas_call | solution.py:357
  31.7 2.2 %shard_map.113 = (f32[512,256]{1,0:T(8,128)}, f32[512,256]{1,0:T(8,128)}, f32[512,256]{1,0:T(8,128)}) custom-call(f32[512,256]{1,0:T(8,128)} %get-tuple-element.9.refs_0_, f32[512,256]{1,0:T(8,128)} %get-tuple-element.10.refs_1_, f32[512,256]{1,0:T(8,128)} %get-tuple-element.11.refs_2_), custom_call_target="tpu_custom_call" | custom-call | tf_op jit(solution)/shard_map/pallas_call | solution.py:418
